TPU v7x, 32 devices: a whole 2x2x4 slice. The times are simulated.
32 devices in a mesh: box: 4 (over x, core), dir: 8 (over z, y).
Axes of the slice: x: 2, y: 2, z: 4, core: 2. Of those that a mesh axis runs over, the one named last changes fastest.
Arguments:
- fine_pattern: bfloat16 [128, 2, 16, 8192], P(('box', 'dir')), may hold values from -6 to 6
- fine_interp: bfloat16 [32, 384, 896], P('dir'), may hold values from -0.3125 to 0.3125
- mid_interp: bfloat16 [32, 1024, 3328], P('dir'), may hold values from -0.1875 to 0.1875
- fine_angle: float32 [8, 28672], P(None, 'dir'), may hold values from -3.140625 to 3.140625
- top_angle: float32 [8, 106496], P(None, 'dir'), may hold values from -3.140625 to 3.140625
- translator: bfloat16 [64, 2, 106496], P(None, None, 'dir'), may hold values from -1 to 1
- fine_position: int32 [128], replicated, may hold values from 0 to 7
- mid_position: int32 [32], replicated, may hold values from 0 to 7
- fine_parent: int32 [128], replicated, may hold values from 0 to 31, as said below
- mid_parent: int32 [32], replicated, may hold values from 0 to 7, as said below
- pair_target: int32 [64], replicated, may hold values from 0 to 7
- pair_source: int32 [64], replicated, may hold values from 0 to 7
- pair_kind: int32 [64], replicated, may hold values from 0 to 63
Outputs:
- top_incoming: float32 [8, 2, 16, 106496], P('box', None, None, 'dir')
- mid_incoming: float32 [32, 2, 16, 28672], P('box', None, None, 'dir')
Inputs may be any that keep to these rules, and one draw needn't show every extreme that they name: `fine_parent`: for every k, the fine boxes k * 32 to (k + 1) * 32 - 1 have their parents among the middle boxes k * 8 to (k + 1) * 8 - 1, and every middle box has exactly 4 children. `mid_parent`: for every k, the middle boxes k * 8 to (k + 1) * 8 - 1 have their parents among the top boxes k * 2 to (k + 1) * 2 - 1, and every top box has exactly 4 children.
All inputs are finite; a program needn't handle non-finite values.
Results may differ from a plain program's by a relative error of at most 0.0072.
Values may be sent and summed in bfloat16 or wider, within the bound.
A program may use at most 128 MiB of HBM per device.

v0:
```python
import functools

import jax
import jax.numpy as jnp
from jax import lax
from jax.experimental import pallas as pl
from jax.experimental.pallas import tpu as pltpu
from jax.sharding import PartitionSpec as P

MESH = pl.DeviceIdType.MESH
F32 = jnp.float32
BF16 = jnp.bfloat16
EDGE = 128


def visit_order(sectors):
    if sectors <= 2:
        return list(range(sectors))
    return list(range(1, sectors - 1)) + [0, sectors - 1]


def down_order(sectors):
    if sectors <= 2:
        return list(range(sectors))
    inner = list(range(1, sectors - 1))
    return inner[:1] + [0, sectors - 1] + inner[1:]


def kernel(
    fchild,
    mchild,
    mrank,
    fine,
    fint,
    mint,
    trans,
    fcos,
    fsin,
    tcos,
    tsin,
    cnt,
    top_out,
    mid_out,
    xf,
    fhl,
    fhr,
    wf,
    wm,
    xm,
    mhl,
    mhr,
    xs,
    gat,
    traw,
    tview,
    cpl,
    spread,
    acc,
    stage,
    esl,
    esr,
    erl,
    err,
    a2a_send,
    a2a_recv,
    own_sem,
    wf_sem,
    wm_sem,
    tr_sem,
    fh_send,
    fh_recv,
    mh_send,
    mh_recv,
    g_send,
    g_recv,
    ed_send,
    ed_recv,
    out_sem,
):
    nd = lax.axis_size("dir")
    nb = lax.axis_size("box")
    me = lax.axis_index("dir")
    box = lax.axis_index("box")
    chips = nb // 2
    sectors, kf, ms = fint.shape
    km, ts = mint.shape[1:]
    fl, _, rhs, fdir = fine.shape
    fg, _, _, fblock = xf.shape
    fs = fblock // sectors
    halo = (kf - fs) // 2
    mg = xm.shape[0]
    tg = mg // 4
    nt = tg * nb
    rows = 2 * rhs
    pad = EDGE - halo
    spanf = fs + 2 * EDGE
    spanm = ms + 2 * EDGE
    left = lax.rem(me + nd - 1, nd)
    right = lax.rem(me + 1, nd)
    sib = box + 1 - 2 * lax.rem(box, 2)
    across = [lax.rem(box + 2 * k, nb) for k in range(1, chips)]
    peers = [lax.rem(me + k, nd) for k in range(1, nd)]

    barrier = pltpu.get_barrier_semaphore()
    for p in peers:
        pl.semaphore_signal(barrier, inc=1, device_id={"dir": p}, device_id_type=MESH)
    for p in [sib] + across:
        pl.semaphore_signal(barrier, inc=1, device_id={"box": p}, device_id_type=MESH)
    pl.semaphore_wait(barrier, len(peers) + 1 + len(across))

    def columns(d):
        return pl.ds(pl.multiple_of(d * fblock, 128), fblock)

    mine = pl.ds(me * fl, fl)
    a2a = [
        pltpu.make_async_remote_copy(
            src_ref=fine.at[:, :, :, columns(p)],
            dst_ref=xf.at[mine],
            send_sem=a2a_send.at[k],
            recv_sem=a2a_recv.at[k],
            device_id={"dir": p},
            device_id_type=MESH,
        )
        for k, p in enumerate(peers)
    ]
    for c in a2a:
        c.start()
    own = pltpu.make_async_copy(fine.at[:, :, :, columns(me)], xf.at[mine], own_sem)
    own.start()

    wf_copies = [
        pltpu.make_async_copy(fint.at[s], wf.at[s, pl.ds(pad, kf)], wf_sem.at[s])
        for s in range(sectors)
    ]
    wm_copies = [
        pltpu.make_async_copy(mint.at[s], wm.at[s, pl.ds(pad, km)], wm_sem.at[s])
        for s in range(sectors)
    ]
    for c in wf_copies + wm_copies:
        c.start()

    for s in range(sectors):
        for buf, k, n in ((wf, kf, ms), (wm, km, ts)):
            buf[s, pl.ds(0, pad), :] = jnp.zeros((pad, n), BF16)
            buf[s, pl.ds(pad + k, pad), :] = jnp.zeros((pad, n), BF16)
    acc[...] = jnp.zeros(acc.shape, F32)

    kinds = trans.shape[0]
    for s in range(sectors):
        fetch = pltpu.make_async_copy(
            trans.at[:, :, pl.ds(s * ts, ts)], traw, tr_sem.at[s]
        )
        fetch.start()
        fetch.wait()

        @pl.loop(0, kinds // 8)
        def _(g, s=s):
            group = [traw[g * 8 + i].astype(F32) for i in range(8)]
            tview[
                pl.ds(pl.multiple_of(g * 16, 16), 16), pl.ds(s * ts, ts)
            ] = jnp.concatenate(group, axis=0).astype(BF16)

    own.wait()
    for c in a2a:
        c.wait_recv()

    def neighbour_copies(src_l, src_r, dst_l, dst_r, send, recv):
        return [
            pltpu.make_async_remote_copy(
                src_ref=src_r,
                dst_ref=dst_l,
                send_sem=send.at[0],
                recv_sem=recv.at[0],
                device_id={"dir": right},
                device_id_type=MESH,
            ),
            pltpu.make_async_remote_copy(
                src_ref=src_l,
                dst_ref=dst_r,
                send_sem=send.at[1],
                recv_sem=recv.at[1],
                device_id={"dir": left},
                device_id_type=MESH,
            ),
        ]

    fine_edges = neighbour_copies(
        xf.at[:, :, :, pl.ds(0, EDGE)],
        xf.at[:, :, :, pl.ds(fblock - EDGE, EDGE)],
        fhl,
        fhr,
        fh_send,
        fh_recv,
    )
    for c in fine_edges:
        c.start()

    def window(core, low, high, index, s, width):
        begin = s * width - EDGE
        end = (s + 1) * width + EDGE
        total = core.shape[3]
        parts = []
        if begin < 0:
            parts.append(low[index])
        first, last = max(begin, 0), min(end, total)
        parts.append(core[index, :, :, pl.ds(first, last - first)])
        if end > total:
            parts.append(high[index])
        parts = [p.reshape(rows, p.shape[-1]) for p in parts]
        return parts[0] if len(parts) == 1 else jnp.concatenate(parts, axis=1)

    halo_seen = False
    for s in visit_order(sectors):
        if (s == 0 or s == sectors - 1) and not halo_seen:
            for c in fine_edges:
                c.wait_recv()
            halo_seen = True
        wf_copies[s].wait()

        @pl.loop(0, mg)
        def _(m, s=s):
            gathered = jnp.concatenate(
                [window(xf, fhl, fhr, fchild[m * 4 + j], s, fs) for j in range(4)], axis=0
            )
            coarse = jnp.dot(gathered, wf[s], preferred_element_type=F32)
            coarse = coarse.astype(BF16).astype(F32)
            re = im = None
            for j in range(4):
                turn = pl.ds(m * 4 + j, 1)
                c = fcos[turn, pl.ds(s * ms, ms)]
                d = fsin[turn, pl.ds(s * ms, ms)]
                u = coarse[j * rows : j * rows + rhs]
                v = coarse[j * rows + rhs : (j + 1) * rows]
                a, b = c * u - d * v, d * u + c * v
                re, im = (a, b) if re is None else (re + a, im + b)
            xm[m, 0, :, pl.ds(s * ms, ms)] = re.astype(BF16)
            xm[m, 1, :, pl.ds(s * ms, ms)] = im.astype(BF16)

    mblock = sectors * ms
    mid_edges = neighbour_copies(
        xm.at[:, :, :, pl.ds(0, EDGE)],
        xm.at[:, :, :, pl.ds(mblock - EDGE, EDGE)],
        mhl,
        mhr,
        mh_send,
        mh_recv,
    )
    for c in mid_edges:
        c.start()

    tile = 256 if ts % 256 == 0 else 128
    tiles = ts // tile

    def near(s):
        return pltpu.make_async_remote_copy(
            src_ref=gat.at[s, box],
            dst_ref=gat.at[s, box],
            send_sem=g_send.at[s, 0],
            recv_sem=g_recv.at[s, 0],
            device_id={"box": sib},
            device_id_type=MESH,
        )

    def far(s, k):
        return pltpu.make_async_remote_copy(
            src_ref=gat.at[s, box],
            dst_ref=gat.at[s, box],
            send_sem=g_send.at[s, 1 + k],
            recv_sem=g_recv.at[s, 1 + k],
            device_id={"box": across[k]},
            device_id_type=MESH,
        )

    def pass_on(s, k):
        origin = lax.rem(box + nb - 2 * (k + 1), nb)
        return pltpu.make_async_remote_copy(
            src_ref=gat.at[s, origin],
            dst_ref=gat.at[s, origin],
            send_sem=g_send.at[s, chips + k],
            recv_sem=g_recv.at[s, chips + k],
            device_id={"box": sib},
            device_id_type=MESH,
        )

    halo_seen = False
    for s in visit_order(sectors):
        if (s == 0 or s == sectors - 1) and not halo_seen:
            for c in mid_edges:
                c.wait_recv()
            halo_seen = True
        wm_copies[s].wait()

        @pl.loop(0, mg)
        def _(i, s=s):
            xs[pl.ds(pl.multiple_of(i * rows, rows), rows), :] = window(
                xm, mhl, mhr, mchild[i], s, ms
            )

        @pl.loop(0, tiles)
        def _(n, s=s):
            here = pl.ds(pl.multiple_of(n * tile, tile), tile)
            whole = pl.ds(pl.multiple_of(s * ts + n * tile, 128), tile)
            coarse = jnp.dot(xs[...], wm[s, :, here], preferred_element_type=F32)
            coarse = coarse.astype(BF16).astype(F32)
            for t in range(tg):
                re = im = None
                for j in range(4):
                    i = t * 4 + j
                    turn = pl.ds(i, 1)
                    c = tcos[turn, whole]
                    d = tsin[turn, whole]
                    u = coarse[i * rows : i * rows + rhs]
                    v = coarse[i * rows + rhs : (i + 1) * rows]
                    a, b = c * u - d * v, d * u + c * v
                    re, im = (a, b) if re is None else (re + a, im + b)
                gat[s, box, t, 0, :, here] = re.astype(BF16)
                gat[s, box, t, 1, :, here] = im.astype(BF16)

        for k in range(chips - 1):
            far(s, k).start()
        near(s).start()

    order = down_order(sectors)
    edge_copies = neighbour_copies(esl, esr, erl, err, ed_send, ed_recv)
    out_copies = []
    for step, s in enumerate(order):
        for k in range(chips - 1):
            far(s, k).wait_recv()
            pass_on(s, k).start()
        near(s).wait_recv()
        for k in range(chips - 1):
            pass_on(s, k).wait_recv()
        slot = step % 2
        if step >= 2:
            out_copies[step - 2].wait()

        @pl.loop(0, tiles)
        def _(n, s=s, slot=slot):
            here = pl.ds(pl.multiple_of(n * tile, tile), tile)
            whole = pl.ds(pl.multiple_of(s * ts + n * tile, 128), tile)
            product = jnp.dot(cnt[...], tview[:, whole], preferred_element_type=F32)
            cpl[...] = product.astype(BF16).astype(F32)
            for t in range(tg):

                def add(u, total, t=t):
                    re, im = total
                    origin = u // tg
                    q = u - origin * tg
                    c = cpl[pl.ds(2 * (t * nt + u), 1), :]
                    d = cpl[pl.ds(2 * (t * nt + u) + 1, 1), :]
                    a = gat[s, origin, q, 0, :, here].astype(F32)
                    b = gat[s, origin, q, 1, :, here].astype(F32)
                    return re + (c * a - d * b), im + (c * b + d * a)

                total = (jnp.zeros((rhs, tile), F32), jnp.zeros((rhs, tile), F32))
                if nt <= 8:
                    for u in range(nt):
                        total = add(u, total)
                else:
                    total = lax.fori_loop(0, nt, add, total)
                re, im = total
                stage[slot, t, 0, :, here] = re
                stage[slot, t, 1, :, here] = im
                re = re.astype(BF16).astype(F32)
                im = im.astype(BF16).astype(F32)
                for j in range(4):
                    i = t * 4 + j
                    turn = pl.ds(i, 1)
                    c = tcos[turn, whole]
                    d = tsin[turn, whole]
                    spread[pl.ds(i * rows, rhs), :] = (c * re + d * im).astype(BF16)
                    spread[pl.ds(i * rows + rhs, rhs), :] = (c * im - d * re).astype(BF16)
            acc[:, :, pl.ds(s * ms, spanm)] += lax.dot_general(
                spread[...],
                wm[s, :, here],
                (((1,), (1,)), ((), ())),
                preferred_element_type=F32,
            ).reshape(mg, rows, spanm)

        out = pltpu.make_async_copy(
            stage.at[slot],
            top_out.at[:, :, :, pl.ds(s * ts, ts)],
            out_sem.at[step],
        )
        out.start()
        out_copies.append(out)
        if set(order[: step + 1]) >= {0, sectors - 1} and not (
            set(order[:step]) >= {0, sectors - 1}
        ):
            esl[...] = acc[:, :, pl.ds(0, EDGE)].astype(BF16)
            esr[...] = acc[:, :, pl.ds(EDGE + mblock, EDGE)].astype(BF16)
            for c in edge_copies:
                c.start()

    for c in edge_copies:
        c.wait_recv()
    acc[:, :, pl.ds(EDGE, EDGE)] += erl[...].astype(F32)
    acc[:, :, pl.ds(mblock, EDGE)] += err[...].astype(F32)

    @pl.loop(0, mg)
    def _(m):
        got = acc[mrank[m], :, pl.ds(EDGE, mblock)]
        mid_out[m] = got.reshape(2, rhs, mblock)

    for c in out_copies[-2:]:
        c.wait()
    for c in a2a + fine_edges + mid_edges + edge_copies:
        c.wait_send()
    for s in range(sectors):
        near(s).wait_send()
        for k in range(chips - 1):
            far(s, k).wait_send()
            pass_on(s, k).wait_send()


def ranking(parents, positions):
    count = parents.shape[0]
    index = jnp.arange(count, dtype=jnp.int32)
    before = (parents[None, :] < parents[:, None]) | (
        (parents[None, :] == parents[:, None]) & (index[None, :] < index[:, None])
    )
    rank = jnp.sum(before.astype(jnp.int32), axis=1)
    chosen = (rank[None, :] == index[:, None]).astype(jnp.int32)
    child = jnp.sum(chosen * index[None, :], axis=1)
    return rank, child, jnp.sum(chosen * positions[None, :], axis=1)


def pair_counts(
    pair_target, pair_source, pair_kind, target_base, target_count, source_count, kind_count
):
    inside = (pair_target >= target_base) & (pair_target < target_base + target_count)
    slot_index = jnp.where(inside, (pair_target - target_base) * source_count + pair_source, -1)
    onehot_pair = (
        slot_index[:, None] == jnp.arange(target_count * source_count, dtype=jnp.int32)[None, :]
    ).astype(BF16)
    onehot_kind = (pair_kind[:, None] == jnp.arange(kind_count, dtype=jnp.int32)[None, :]).astype(
        BF16
    )
    return jnp.dot(onehot_pair.T, onehot_kind, preferred_element_type=F32).astype(BF16)


def per_device(
    fine_pattern,
    fine_interp,
    mid_interp,
    fine_angle,
    top_angle,
    translator,
    fine_position,
    mid_position,
    fine_parent,
    mid_parent,
    pair_target,
    pair_source,
    pair_kind,
):
    box = lax.axis_index("box")
    nd = lax.axis_size("dir")
    nb = lax.axis_size("box")
    fl, _, rhs, fdir = fine_pattern.shape
    sectors, kf, ms = fine_interp.shape
    km, ts = mid_interp.shape[1:]
    kinds = translator.shape[0]
    fg = fl * nd
    mg = fg // 4
    tg = mg // 4
    nt = tg * nb
    rows = 2 * rhs
    fblock = fdir // nd
    fs = fblock // sectors
    mblock = sectors * ms
    tblock = sectors * ts
    chips = nb // 2
    tile = 256 if ts % 256 == 0 else 128

    def local(array, count):
        return lax.dynamic_slice_in_dim(array, box * count, count)

    _, fchild, fposc = ranking(local(fine_parent, fg), local(fine_position, fg))
    mrank, mchild, mposc = ranking(local(mid_parent, mg), local(mid_position, mg))
    fine_turns = fine_angle[fposc]
    top_turns = top_angle[mposc]
    counts = pair_counts(pair_target, pair_source, pair_kind, box * tg, tg, nt, kinds)
    eye = jnp.eye(2, dtype=BF16)
    cnt = (counts[:, None, :, None] * eye[None, :, None, :]).reshape(tg * nt * 2, kinds * 2)

    vmem = pl.BlockSpec(memory_space=pltpu.VMEM)
    smem = pl.BlockSpec(memory_space=pltpu.SMEM)
    hbm = pl.BlockSpec(memory_space=pl.ANY)
    dma = pltpu.SemaphoreType.DMA
    paths = 2 * chips - 1
    return pl.pallas_call(
        kernel,
        out_shape=(
            jax.ShapeDtypeStruct((tg, 2, rhs, tblock), F32),
            jax.ShapeDtypeStruct((mg, 2, rhs, mblock), F32),
        ),
        in_specs=[smem] * 3 + [hbm] * 4 + [vmem] * 5,
        out_specs=(hbm, vmem),
        scratch_shapes=[
            pltpu.VMEM((fg, 2, rhs, fblock), BF16),
            pltpu.VMEM((fg, 2, rhs, EDGE), BF16),
            pltpu.VMEM((fg, 2, rhs, EDGE), BF16),
            pltpu.VMEM((sectors, fs + 2 * EDGE, ms), BF16),
            pltpu.VMEM((sectors, ms + 2 * EDGE, ts), BF16),
            pltpu.VMEM((mg, 2, rhs, mblock), BF16),
            pltpu.VMEM((mg, 2, rhs, EDGE), BF16),
            pltpu.VMEM((mg, 2, rhs, EDGE), BF16),
            pltpu.VMEM((mg * rows, ms + 2 * EDGE), BF16),
            pltpu.VMEM((sectors, nb, tg, 2, rhs, ts), BF16),
            pltpu.VMEM((kinds, 2, ts), BF16),
            pltpu.VMEM((2 * kinds, tblock), BF16),
            pltpu.VMEM((tg * nt * 2, tile), F32),
            pltpu.VMEM((mg * rows, tile), BF16),
            pltpu.VMEM((mg, rows, mblock + 2 * EDGE), F32),
            pltpu.VMEM((2, tg, 2, rhs, ts), F32),
            pltpu.VMEM((mg, rows, EDGE), BF16),
            pltpu.VMEM((mg, rows, EDGE), BF16),
            pltpu.VMEM((mg, rows, EDGE), BF16),
            pltpu.VMEM((mg, rows, EDGE), BF16),
            dma((nd - 1,)),
            dma((nd - 1,)),
            dma,
            dma((sectors,)),
            dma((sectors,)),
            dma((sectors,)),
            dma((2,)),
            dma((2,)),
            dma((2,)),
            dma((2,)),
            dma((sectors, paths)),
            dma((sectors, paths)),
            dma((2,)),
            dma((2,)),
            dma((sectors,)),
        ],
        compiler_params=pltpu.CompilerParams(
            collective_id=0, has_side_effects=True, vmem_limit_bytes=63 * 1024 * 1024
        ),
    )(
        fchild,
        mchild,
        mrank,
        fine_pattern,
        fine_interp,
        mid_interp,
        translator,
        jnp.cos(fine_turns),
        jnp.sin(fine_turns),
        jnp.cos(top_turns),
        jnp.sin(top_turns),
        cnt,
    )


def solution(mesh):
    placed = (
        P(("box", "dir"), None, None, None),
        P("dir", None, None),
        P("dir", None, None),
        P(None, "dir"),
        P(None, "dir"),
        P(None, None, "dir"),
        P(),
        P(),
        P(),
        P(),
        P(),
        P(),
        P(),
    )
    return jax.shard_map(
        per_device,
        mesh=mesh,
        in_specs=placed,
        out_specs=(P("box", None, None, "dir"), P("box", None, None, "dir")),
        check_vma=False,
    )
```

profile of v0, /device:TPU:0, one launch (start us, length us, event | category | flops | bytes accessed | tf_op | source)
XLA Modules:
  0.0 156.1 jit_solution(3943247192322647627)
XLA Ops:
  0.6 0.0 copy-start
  0.6 0.0 copy-start.1
  0.7 0.7 and_select_fusion
  1.4 0.7 dynamic_slice.14
  2.1 0.7 dynamic_slice.12
  2.9 0.2 convert_reduce_fusion
  3.0 0.7 select_reduce_fusion
  3.7 0.7 dynamic_slice.15
  4.4 0.7 dynamic_slice.13
  5.1 0.2 convert_reduce_fusion.1.mrank
  5.3 0.7 select_reduce_fusion.2
  6.1 0.9 convolution_convert_fusion
  7.0 0.0 copy-done
  7.0 0.7 gather_fusion.1
  7.7 2.4 %fusion.9 = (f32[8,13312]{1,0:T(8,128)}, f32[8,13312]{1,0:T(8,128)}) fusion(f32[8,13312]{1,0:T(8,128)S(1)} %gather_fusion.1), kind=kLoop, calls=%fused_computation.31 | loop fusion | bytes 1277952 | tf_op jit(solution)/shard_map/sin | solution.py:551
  10.1 0.0 copy-done.1
  10.1 0.7 gather_fusion
  10.9 0.0 copy-done.3
  10.9 2.4 %fusion.8 = (f32[32,3584]{1,0:T(8,128)}, f32[32,3584]{1,0:T(8,128)}) fusion(f32[32,3584]{1,0:T(8,128)S(1)} %gather_fusion), kind=kLoop, calls=%fused_computation.30 | loop fusion | bytes 1376256 | tf_op jit(solution)/shard_map/sin | solution.py:549
  13.3 0.2 broadcast_multiply_fusion
  13.5 1.2 mul.76.cnt
  14.7 135.4 %shard_map.140 = (f32[2,2,16,13312]{3,2,1,0:T(8,128)}, f32[8,2,16,3584]{3,2,1,0:T(8,128)}) custom-call(s32[32]{0:T(128)} %get-tuple-element.5.fchild, s32[8]{0:T(128)} %get-tuple-element.3.mchild, s32[8]{0:T(128)} %copy-done.3, bf16[4,2,16,8192]{3,2,1,0:T(8,128)(2,1)} %fine.1, bf16[4,384,896]{2,1,0:T(8,128)(2,1)} %fint.1, bf16[4,1024,3328]{2,1,0:T(8,128)(2,1)} %mint.1, ...), custom_call_target="tpu_custom_call" | custom-call | tf_op jit(solution)/shard_map/pallas_call | solution.py:492
  150.1 4.1 %copy.17 = f32[2,2,16,13312]{3,2,1,0:T(8,128)} copy(f32[2,2,16,13312]{3,2,1,0:T(8,128)} %get-tuple-element.12) | data formatting | bytes 6815744
  154.2 1.8 %copy.18 = f32[8,2,16,3584]{3,2,1,0:T(8,128)} copy(f32[8,2,16,3584]{3,2,1,0:T(8,128)S(1)} %copy-done.2) | data formatting | bytes 7340032
  (8 shorter events, 0.0 us)
Async XLA Ops:
  0.6 6.4 %copy-start = (f32[8,13312]{1,0:T(8,128)S(1)}, f32[8,13312]{1,0:T(8,128)}, u32[]{:S(2)}) copy-start(f32[8,13312]{1,0:T(8,128)} %param.17) | copy-start | bytes 1277956
  0.6 9.5 %copy-start.1 = (f32[8,3584]{1,0:T(8,128)S(1)}, f32[8,3584]{1,0:T(8,128)}, u32[]{:S(2)}) copy-start(f32[8,3584]{1,0:T(8,128)} %param.16) | copy-start | bytes 344068
  5.3 5.5 %copy-start.3 = (s32[8]{0:T(128)}, s32[8]{0:T(128)S(1)}, u32[]{:S(2)}) copy-start(s32[8]{0:T(128)S(1)} %convert_reduce_fusion.1.mrank) | copy-start | bytes 100
  150.1 4.1 %copy-start.2 = (f32[8,2,16,3584]{3,2,1,0:T(8,128)S(1)}, f32[8,2,16,3584]{3,2,1,0:T(8,128)}, u32[]{:S(2)}) copy-start(f32[8,2,16,3584]{3,2,1,0:T(8,128)} %get-tuple-element.13) | copy-start | bytes 11010052
where the time goes:
time: 158 us; the launch traced here: 156 us
  Pallas kernels  135 us (85%)
  local copies, waits for them, and re-layouts  16.3 us (10%)
  other arithmetic  2.69 us (2%)
    pallas_call x1, Pallas kernels, per_device(): pl.pallas_call(kernel, out_shape=(jax.ShapeDtypeStruct((tg, 2, rhs, tbloc...  135 us
    unnamed x10, local copies, waits for them, and re-layouts  5.97 us

commit v1 on v0

v1 whole, which is shorter than its diff:
```python
import functools

import jax
import jax.numpy as jnp
from jax import lax
from jax.experimental import pallas as pl
from jax.experimental.pallas import tpu as pltpu
from jax.sharding import PartitionSpec as P

MESH = pl.DeviceIdType.MESH
F32 = jnp.float32
BF16 = jnp.bfloat16
EDGE = 128


def visit_order(sectors):
    if sectors <= 2:
        return list(range(sectors))
    return [1, 0, sectors - 1] + list(range(2, sectors - 1))


def circle(angle):
    quarter = angle * 0.25
    x = quarter * quarter
    sine = quarter * (
        1.0 + x * (-1.0 / 6 + x * (1.0 / 120 + x * (-1.0 / 5040 + x * (1.0 / 362880))))
    )
    cosine = 1.0 + x * (
        -0.5 + x * (1.0 / 24 + x * (-1.0 / 720 + x * (1.0 / 40320 - x * (1.0 / 3628800))))
    )
    for _ in range(2):
        sine, cosine = 2.0 * sine * cosine, 1.0 - 2.0 * sine * sine
    return cosine, sine


def kernel(
    child,
    rank,
    fine,
    fint,
    mint,
    trans,
    fang,
    tang,
    fpos,
    mpos,
    cnt,
    top_out,
    mid_out,
    fcos,
    fsin,
    tcos,
    tsin,
    xf,
    fhl,
    fhr,
    wf,
    wm,
    xm,
    mhl,
    mhr,
    xs,
    gat,
    traw,
    tview,
    cpl,
    turned,
    spread,
    acc,
    stage,
    esl,
    esr,
    erl,
    err,
    a2a_send,
    a2a_recv,
    own_sem,
    wf_sem,
    wm_sem,
    tr_sem,
    fh_send,
    fh_recv,
    mh_send,
    mh_recv,
    g_send,
    g_recv,
    ed_send,
    ed_recv,
    out_sem,
    mid_sem,
):
    nd = lax.axis_size("dir")
    nb = lax.axis_size("box")
    me = lax.axis_index("dir")
    box = lax.axis_index("box")
    chips = nb // 2
    sectors, kf, ms = fint.shape
    km, ts = mint.shape[1:]
    fl, _, rhs, fdir = fine.shape
    fg, _, _, fblock = xf.shape
    fs = fblock // sectors
    halo = (kf - fs) // 2
    mg = xm.shape[0]
    tg = mg // 4
    nt = tg * nb
    rows = 2 * rhs
    pad = EDGE - halo
    spanf = fs + 2 * EDGE
    spanm = ms + 2 * EDGE
    left = lax.rem(me + nd - 1, nd)
    right = lax.rem(me + 1, nd)
    sib = box + 1 - 2 * lax.rem(box, 2)
    across = [lax.rem(box + 2 * k, nb) for k in range(1, chips)]
    peers = [lax.rem(me + k, nd) for k in range(1, nd)]

    barrier = pltpu.get_barrier_semaphore()
    for p in peers:
        pl.semaphore_signal(barrier, inc=1, device_id={"dir": p}, device_id_type=MESH)
    for p in [sib] + across:
        pl.semaphore_signal(barrier, inc=1, device_id={"box": p}, device_id_type=MESH)
    pl.semaphore_wait(barrier, len(peers) + 1 + len(across))

    def columns(d):
        return pl.ds(pl.multiple_of(d * fblock, 128), fblock)

    mine = pl.ds(me * fl, fl)
    a2a = [
        pltpu.make_async_remote_copy(
            src_ref=fine.at[:, :, :, columns(p)],
            dst_ref=xf.at[mine],
            send_sem=a2a_send.at[k],
            recv_sem=a2a_recv.at[k],
            device_id={"dir": p},
            device_id_type=MESH,
        )
        for k, p in enumerate(peers)
    ]
    for c in a2a:
        c.start()
    own = pltpu.make_async_copy(fine.at[:, :, :, columns(me)], xf.at[mine], own_sem)
    own.start()

    wf_copies = [
        pltpu.make_async_copy(fint.at[s], wf.at[s, pl.ds(pad, kf)], wf_sem.at[s])
        for s in range(sectors)
    ]
    wm_copies = [
        pltpu.make_async_copy(mint.at[s], wm.at[s, pl.ds(pad, km)], wm_sem.at[s])
        for s in range(sectors)
    ]
    for c in wf_copies + wm_copies:
        c.start()

    for s in range(sectors):
        for buf, k, n in ((wf, kf, ms), (wm, km, ts)):
            buf[s, pl.ds(0, pad), :] = jnp.zeros((pad, n), BF16)
            buf[s, pl.ds(pad + k, pad), :] = jnp.zeros((pad, n), BF16)
    acc[...] = jnp.zeros(acc.shape, F32)

    kinds = trans.shape[0]
    for s in range(sectors):
        fetch = pltpu.make_async_copy(
            trans.at[:, :, pl.ds(s * ts, ts)], traw, tr_sem.at[s]
        )
        fetch.start()
        fetch.wait()

        @pl.loop(0, kinds // 8)
        def _(g, s=s):
            group = [traw[g * 8 + i].astype(F32) for i in range(8)]
            tview[
                pl.ds(pl.multiple_of(g * 16, 16), 16), pl.ds(s * ts, ts)
            ] = jnp.concatenate(group, axis=0).astype(BF16)

    for angles, places, cosines, sines, width in (
        (fang, fpos, fcos, fsin, 128),
        (tang, mpos, tcos, tsin, 256),
    ):

        @pl.loop(0, angles.shape[1] // width)
        def _(n, angles=angles, places=places, cosines=cosines, sines=sines, width=width):
            here = pl.ds(pl.multiple_of(n * width, width), width)
            table = angles[:, here]
            place = jnp.broadcast_to(places[...], (places.shape[0], width))
            angle = jnp.zeros(place.shape, F32)
            for p in range(table.shape[0]):
                row = jnp.broadcast_to(table[p : p + 1], place.shape)
                angle = jnp.where(place == p, row, angle)
            cosine, sine = circle(angle)
            cosines[:, here] = cosine
            sines[:, here] = sine

    own.wait()
    for c in a2a:
        c.wait_recv()

    def neighbour_copies(src_l, src_r, dst_l, dst_r, send, recv):
        return [
            pltpu.make_async_remote_copy(
                src_ref=src_r,
                dst_ref=dst_l,
                send_sem=send.at[0],
                recv_sem=recv.at[0],
                device_id={"dir": right},
                device_id_type=MESH,
            ),
            pltpu.make_async_remote_copy(
                src_ref=src_l,
                dst_ref=dst_r,
                send_sem=send.at[1],
                recv_sem=recv.at[1],
                device_id={"dir": left},
                device_id_type=MESH,
            ),
        ]

    fine_edges = neighbour_copies(
        xf.at[:, :, :, pl.ds(0, EDGE)],
        xf.at[:, :, :, pl.ds(fblock - EDGE, EDGE)],
        fhl,
        fhr,
        fh_send,
        fh_recv,
    )
    for c in fine_edges:
        c.start()

    def window(core, low, high, index, s, width):
        begin = s * width - EDGE
        end = (s + 1) * width + EDGE
        total = core.shape[3]
        parts = []
        if begin < 0:
            parts.append(low[index])
        first, last = max(begin, 0), min(end, total)
        parts.append(core[index, :, :, pl.ds(first, last - first)])
        if end > total:
            parts.append(high[index])
        parts = [p.reshape(rows, p.shape[-1]) for p in parts]
        return parts[0] if len(parts) == 1 else jnp.concatenate(parts, axis=1)

    group = 2 if mg % 2 == 0 else 1
    halo_seen = False
    for s in visit_order(sectors):
        if (s == 0 or s == sectors - 1) and not halo_seen:
            for c in fine_edges:
                c.wait_recv()
            halo_seen = True
        wf_copies[s].wait()

        @pl.loop(0, mg // group)
        def _(g, s=s):
            begin = g * 4 * group
            gathered = jnp.concatenate(
                [window(xf, fhl, fhr, child[begin + i], s, fs) for i in range(4 * group)], axis=0
            )
            coarse = jnp.dot(gathered, wf[s], preferred_element_type=F32)
            coarse = coarse.astype(BF16).astype(F32)
            for h in range(group):
                re = im = None
                for i in range(4 * h, 4 * h + 4):
                    turn = pl.ds(begin + i, 1)
                    c = fcos[turn, pl.ds(s * ms, ms)]
                    d = fsin[turn, pl.ds(s * ms, ms)]
                    u = coarse[i * rows : i * rows + rhs]
                    v = coarse[i * rows + rhs : (i + 1) * rows]
                    a, b = c * u - d * v, d * u + c * v
                    re, im = (a, b) if re is None else (re + a, im + b)
                xm[g * group + h, 0, :, pl.ds(s * ms, ms)] = re.astype(BF16)
                xm[g * group + h, 1, :, pl.ds(s * ms, ms)] = im.astype(BF16)

    mblock = sectors * ms
    mid_edges = neighbour_copies(
        xm.at[:, :, :, pl.ds(0, EDGE)],
        xm.at[:, :, :, pl.ds(mblock - EDGE, EDGE)],
        mhl,
        mhr,
        mh_send,
        mh_recv,
    )
    for c in mid_edges:
        c.start()

    tile = 256 if ts % 256 == 0 else 128
    tiles = ts // tile

    first = (tiles + 1) // 2
    halves = [(0, first)] + ([(first, tiles)] if first < tiles else [])

    def exchange(s, h, origin, path, target):
        low, high = halves[h]
        block = gat.at[s, origin, :, :, :, pl.ds(low * tile, (high - low) * tile)]
        return pltpu.make_async_remote_copy(
            src_ref=block,
            dst_ref=block,
            send_sem=g_send.at[2 * s + h, path],
            recv_sem=g_recv.at[2 * s + h, path],
            device_id={"box": target},
            device_id_type=MESH,
        )

    def near(s, h):
        return exchange(s, h, box, 0, sib)

    def far(s, h, k):
        return exchange(s, h, box, 1 + k, across[k])

    def pass_on(s, h, k):
        return exchange(s, h, lax.rem(box + nb - 2 * (k + 1), nb), chips + k, sib)

    halo_seen = False
    for s in visit_order(sectors):
        if (s == 0 or s == sectors - 1) and not halo_seen:
            for c in mid_edges:
                c.wait_recv()
            halo_seen = True
        wm_copies[s].wait()

        @pl.loop(0, mg)
        def _(i, s=s):
            xs[pl.ds(pl.multiple_of(i * rows, rows), rows), :] = window(
                xm, mhl, mhr, child[fg + i], s, ms
            )

        for h in range(len(halves)):

            @pl.loop(*halves[h])
            def _(n, s=s):
                here = pl.ds(pl.multiple_of(n * tile, tile), tile)
                whole = pl.ds(pl.multiple_of(s * ts + n * tile, 128), tile)
                coarse = jnp.dot(xs[...], wm[s, :, here], preferred_element_type=F32)
                coarse = coarse.astype(BF16).astype(F32)
                for t in range(tg):
                    re = im = None
                    for j in range(4):
                        i = t * 4 + j
                        turn = pl.ds(i, 1)
                        c = tcos[turn, whole]
                        d = tsin[turn, whole]
                        u = coarse[i * rows : i * rows + rhs]
                        v = coarse[i * rows + rhs : (i + 1) * rows]
                        a, b = c * u - d * v, d * u + c * v
                        re, im = (a, b) if re is None else (re + a, im + b)
                    gat[s, box, t, 0, :, here] = re.astype(BF16)
                    gat[s, box, t, 1, :, here] = im.astype(BF16)

            for k in range(chips - 1):
                far(s, h, k).start()
            near(s, h).start()

    order = visit_order(sectors)
    edge_copies = neighbour_copies(esl, esr, erl, err, ed_send, ed_recv)
    out_copies = []
    mfirst = rank.shape[0] - nb * mg + box * mg
    for step, s in enumerate(order):
        slot = step % 2
        if step >= 2:
            out_copies[step - 2].wait()
        for h in range(len(halves)):
            for k in range(chips - 1):
                far(s, h, k).wait_recv()
                pass_on(s, h, k).start()
            near(s, h).wait_recv()
            for k in range(chips - 1):
                pass_on(s, h, k).wait_recv()

            @pl.loop(*halves[h])
            def _(n, s=s, slot=slot):
                here = pl.ds(pl.multiple_of(n * tile, tile), tile)
                whole = pl.ds(pl.multiple_of(s * ts + n * tile, 128), tile)
                product = jnp.dot(cnt[...], tview[:, whole], preferred_element_type=F32)
                cpl[...] = product.astype(BF16).astype(F32)
                for t in range(tg):

                    def add(u, total, t=t):
                        re, im = total
                        origin = u // tg
                        q = u - origin * tg
                        c = cpl[pl.ds(2 * (t * nt + u), 1), :]
                        d = cpl[pl.ds(2 * (t * nt + u) + 1, 1), :]
                        a = gat[s, origin, q, 0, :, here].astype(F32)
                        b = gat[s, origin, q, 1, :, here].astype(F32)
                        return re + (c * a - d * b), im + (c * b + d * a)

                    total = (jnp.zeros((rhs, tile), F32), jnp.zeros((rhs, tile), F32))
                    if nt <= 8:
                        for u in range(nt):
                            total = add(u, total)
                    else:
                        total = lax.fori_loop(0, nt, add, total)
                    re, im = total
                    stage[slot, t, 0, :, here] = re
                    stage[slot, t, 1, :, here] = im
                    re = re.astype(BF16).astype(F32)
                    im = im.astype(BF16).astype(F32)
                    for j in range(4):
                        i = t * 4 + j
                        turn = pl.ds(i, 1)
                        c = tcos[turn, whole]
                        d = tsin[turn, whole]
                        turned[i, 0] = (c * re + d * im).astype(BF16)
                        turned[i, 1] = (c * im - d * re).astype(BF16)
                for m in range(mg):
                    spread[pl.ds(m * rows, rows), :] = turned[
                        rank[mfirst + m]
                    ].reshape(rows, tile)
                acc[:, :, :, pl.ds(s * ms, spanm)] += lax.dot_general(
                    spread[...],
                    wm[s, :, here],
                    (((1,), (1,)), ((), ())),
                    preferred_element_type=F32,
                ).reshape(mg, 2, rhs, spanm)

        out = pltpu.make_async_copy(
            stage.at[slot],
            top_out.at[:, :, :, pl.ds(s * ts, ts)],
            out_sem.at[step],
        )
        out.start()
        out_copies.append(out)
        if set(order[: step + 1]) >= {0, sectors - 1} and not (
            set(order[:step]) >= {0, sectors - 1}
        ):
            esl[...] = acc[:, :, :, pl.ds(0, EDGE)].astype(BF16)
            esr[...] = acc[:, :, :, pl.ds(EDGE + mblock, EDGE)].astype(BF16)
            for c in edge_copies:
                c.start()

    for c in edge_copies:
        c.wait_recv()
    acc[:, :, :, pl.ds(EDGE, EDGE)] += erl[...].astype(F32)
    acc[:, :, :, pl.ds(mblock, EDGE)] += err[...].astype(F32)
    mid_copy = pltpu.make_async_copy(
        acc.at[:, :, :, pl.ds(EDGE, mblock)], mid_out, mid_sem
    )
    mid_copy.start()
    mid_copy.wait()

    for c in out_copies[-2:]:
        c.wait()
    for c in a2a + fine_edges + mid_edges + edge_copies:
        c.wait_send()
    for s in range(sectors):
        for h in range(len(halves)):
            near(s, h).wait_send()
            for k in range(chips - 1):
                far(s, h, k).wait_send()
                pass_on(s, h, k).wait_send()


def ranking(parents, wanted, positions):
    index = jnp.arange(parents.shape[0], dtype=jnp.int32)
    before = (parents[None, :] < parents[:, None]) | (
        (parents[None, :] == parents[:, None]) & (index[None, :] < index[:, None])
    )
    rank = jnp.sum(before.astype(jnp.int32), axis=1)
    chosen = (rank[None, :] == wanted[:, None]).astype(jnp.int32)
    child = jnp.sum(chosen * index[None, :], axis=1)
    return rank, child, jnp.sum(chosen * positions[None, :], axis=1, keepdims=True)


def pair_counts(pair_target, pair_source, pair_kind, base, targets, sources, kinds):
    place = jnp.arange(targets * sources * 2, dtype=jnp.int32)
    column = jnp.arange(kinds * 2, dtype=jnp.int32)
    inside = (pair_target >= base) & (pair_target < base + targets)
    slot = jnp.where(inside, (pair_target - base) * sources + pair_source, -1)
    in_slot = (slot[None, :] == (place // 2)[:, None]).astype(BF16)
    of_kind = (pair_kind[:, None] == (column // 2)[None, :]).astype(BF16)
    counts = jnp.dot(in_slot, of_kind, preferred_element_type=F32)
    same = (place % 2)[:, None] == (column % 2)[None, :]
    return jnp.where(same, counts, 0.0).astype(BF16)


def per_device(
    fine_pattern,
    fine_interp,
    mid_interp,
    fine_angle,
    top_angle,
    translator,
    fine_position,
    mid_position,
    fine_parent,
    mid_parent,
    pair_target,
    pair_source,
    pair_kind,
):
    box = lax.axis_index("box")
    nd = lax.axis_size("dir")
    nb = lax.axis_size("box")
    fl, _, rhs, fdir = fine_pattern.shape
    sectors, kf, ms = fine_interp.shape
    km, ts = mid_interp.shape[1:]
    kinds = translator.shape[0]
    fg = fl * nd
    mg = fg // 4
    tg = mg // 4
    nt = tg * nb
    rows = 2 * rhs
    fblock = fdir // nd
    fs = fblock // sectors
    mblock = sectors * ms
    tblock = sectors * ts
    chips = nb // 2
    tile = 256 if ts % 256 == 0 else 128

    fine_all = fine_parent.shape[0]
    slots = jnp.arange(fg + mg, dtype=jnp.int32)
    start = jnp.where(slots < fg, box * fg, fine_all + box * mg - fg)
    rank, child, place = ranking(
        jnp.concatenate([fine_parent, mid_parent + fine_all]),
        slots + start,
        jnp.concatenate([fine_position, mid_position]),
    )
    index = jnp.arange(rank.shape[0], dtype=jnp.int32)
    inner = jnp.where(index < fine_all, index % fg, (index - fine_all) % mg)
    rank = rank - (index - inner)
    child = child - jnp.where(slots < fg, box * fg, fine_all + box * mg)
    cnt = pair_counts(pair_target, pair_source, pair_kind, box * tg, tg, nt, kinds)

    vmem = pl.BlockSpec(memory_space=pltpu.VMEM)
    smem = pl.BlockSpec(memory_space=pltpu.SMEM)
    hbm = pl.BlockSpec(memory_space=pl.ANY)
    dma = pltpu.SemaphoreType.DMA
    paths = 2 * chips - 1
    return pl.pallas_call(
        kernel,
        out_shape=(
            jax.ShapeDtypeStruct((tg, 2, rhs, tblock), F32),
            jax.ShapeDtypeStruct((mg, 2, rhs, mblock), F32),
        ),
        in_specs=[smem] * 2 + [hbm] * 4 + [vmem] * 5,
        out_specs=(hbm, hbm),
        scratch_shapes=[
            pltpu.VMEM((fg, mblock), F32),
            pltpu.VMEM((fg, mblock), F32),
            pltpu.VMEM((mg, tblock), F32),
            pltpu.VMEM((mg, tblock), F32),
            pltpu.VMEM((fg, 2, rhs, fblock), BF16),
            pltpu.VMEM((fg, 2, rhs, EDGE), BF16),
            pltpu.VMEM((fg, 2, rhs, EDGE), BF16),
            pltpu.VMEM((sectors, fs + 2 * EDGE, ms), BF16),
            pltpu.VMEM((sectors, ms + 2 * EDGE, ts), BF16),
            pltpu.VMEM((mg, 2, rhs, mblock), BF16),
            pltpu.VMEM((mg, 2, rhs, EDGE), BF16),
            pltpu.VMEM((mg, 2, rhs, EDGE), BF16),
            pltpu.VMEM((mg * rows, ms + 2 * EDGE), BF16),
            pltpu.VMEM((sectors, nb, tg, 2, rhs, ts), BF16),
            pltpu.VMEM((kinds, 2, ts), BF16),
            pltpu.VMEM((2 * kinds, tblock), BF16),
            pltpu.VMEM((tg * nt * 2, tile), F32),
            pltpu.VMEM((mg, 2, rhs, tile), BF16),
            pltpu.VMEM((mg * rows, tile), BF16),
            pltpu.VMEM((mg, 2, rhs, mblock + 2 * EDGE), F32),
            pltpu.VMEM((2, tg, 2, rhs, ts), F32),
            pltpu.VMEM((mg, 2, rhs, EDGE), BF16),
            pltpu.VMEM((mg, 2, rhs, EDGE), BF16),
            pltpu.VMEM((mg, 2, rhs, EDGE), BF16),
            pltpu.VMEM((mg, 2, rhs, EDGE), BF16),
            dma((nd - 1,)),
            dma((nd - 1,)),
            dma,
            dma((sectors,)),
            dma((sectors,)),
            dma((sectors,)),
            dma((2,)),
            dma((2,)),
            dma((2,)),
            dma((2,)),
            dma((2 * sectors, paths)),
            dma((2 * sectors, paths)),
            dma((2,)),
            dma((2,)),
            dma((sectors,)),
            dma,
        ],
        compiler_params=pltpu.CompilerParams(
            collective_id=0, has_side_effects=True, vmem_limit_bytes=63 * 1024 * 1024
        ),
    )(
        child,
        rank,
        fine_pattern,
        fine_interp,
        mid_interp,
        translator,
        fine_angle,
        top_angle,
        place[:fg],
        place[fg:],
        cnt,
    )


def solution(mesh):
    placed = (
        P(("box", "dir"), None, None, None),
        P("dir", None, None),
        P("dir", None, None),
        P(None, "dir"),
        P(None, "dir"),
        P(None, None, "dir"),
        P(),
        P(),
        P(),
        P(),
        P(),
        P(),
        P(),
    )
    return jax.shard_map(
        per_device,
        mesh=mesh,
        in_specs=placed,
        out_specs=(P("box", None, None, "dir"), P("box", None, None, "dir")),
        check_vma=False,
    )
```

time: 158 us -> 148 us (0.937)
  local copies, waits for them, and re-layouts: 16.3 us -> 7.39 us
    sin x2 -> x0, local copies, waits for them, and re-layouts: 4.85 us -> none  [the longest x1 2.45 us: per_device(): jnp.sin(top_turns)]
    dynamic_slice x4 -> x0, local copies, waits for them, and re-layouts: 2.91 us -> none  [local(): return lax.dynamic_slice_in_dim(array, box * count, count)]
    pallas_call x1, Pallas kernels: 135 us -> 134 us  [per_device(): pl.pallas_call(kernel, out_shape=(jax.ShapeDtypeStruct((tg, 2, rhs, tbloc...]
    unnamed x10 -> x4, local copies, waits for them, and re-layouts: 5.97 us -> 5.95 us
where the time goes in v1:
time: 148 us; the launch traced here: 147 us
  Pallas kernels  134 us (91%)
  local copies, waits for them, and re-layouts  7.39 us (5%)
  other arithmetic  4.15 us (3%)
    pallas_call x1, Pallas kernels, per_device(): pl.pallas_call(kernel, out_shape=(jax.ShapeDtypeStruct((tg, 2, rhs, tbloc...  134 us
    unnamed x4, local copies, waits for them, and re-layouts  5.95 us

profile of v1, /device:TPU:0, one launch (start us, length us, event | category | flops | bytes accessed | tf_op | source)
XLA Modules:
  0.0 147.4 jit_solution(4153758437050606822)
XLA Ops:
  0.7 0.7 and_select_fusion.2
  1.3 0.7 broadcast_add_fusion
  2.0 0.7 pad_add_fusion
  2.7 0.2 convert_reduce_fusion
  2.8 0.6 fusion.14.rank
  3.4 0.7 pad_add_fusion.1
  4.1 0.2 fusion.4
  4.3 0.5 fusion.16.child
  4.8 0.1 slice_bitcast_fusion
  4.9 0.7 copy.18.mpos
  5.6 1.4 fusion.cnt
  7.0 0.7 copy.17.fpos
  7.7 133.8 %shard_map.140 = (f32[2,2,16,13312]{3,2,1,0:T(8,128)}, f32[8,2,16,3584]{3,2,1,0:T(8,128)}) custom-call(s32[40]{0:T(128)} %fusion.16.child, s32[160]{0:T(256)} %fusion.14.rank, bf16[4,2,16,8192]{3,2,1,0:T(8,128)(2,1)} %fine.1, bf16[4,384,896]{2,1,0:T(8,128)(2,1)} %fint.1, bf16[4,1024,3328]{2,1,0:T(8,128)(2,1)} %mint.1, bf16[64,2,13312]{2,1,0:T(2,128)(2,1)} %trans.1, ...), custom_call_target="tpu_custom_call" | custom-call | tf_op jit(solution)/shard_map/pallas_call | solution.py:527
  141.5 0.0 copy-start
  141.5 4.1 %copy.21 = f32[2,2,16,13312]{3,2,1,0:T(8,128)} copy(f32[2,2,16,13312]{3,2,1,0:T(8,128)} %get-tuple-element.10) | data formatting | bytes 6815744
  145.6 0.0 copy-done
  145.6 1.8 %copy.22 = f32[8,2,16,3584]{3,2,1,0:T(8,128)} copy(f32[8,2,16,3584]{3,2,1,0:T(8,128)S(1)} %copy-done) | data formatting | bytes 7340032
  (4 shorter events, 0.0 us)
Async XLA Ops:
  141.5 4.1 %copy-start = (f32[8,2,16,3584]{3,2,1,0:T(8,128)S(1)}, f32[8,2,16,3584]{3,2,1,0:T(8,128)}, u32[]{:S(2)}) copy-start(f32[8,2,16,3584]{3,2,1,0:T(8,128)} %get-tuple-element.11) | copy-start | bytes 11010052

commit v2 on v1

--- a/solution.py
+++ b/solution.py
@@ -65,6 +65,7 @@
     tview,
     cpl,
     turned,
+    raised,
     spread,
     acc,
     stage,
@@ -284,6 +285,7 @@
     tile = 256 if ts % 256 == 0 else 128
     tiles = ts // tile
 
+    block = 256 if (mg * rows) % 256 == 0 else rows
     first = (tiles + 1) // 2
     halves = [(0, first)] + ([(first, tiles)] if first < tiles else [])
 
@@ -324,12 +326,21 @@
 
         for h in range(len(halves)):
 
-            @pl.loop(*halves[h])
-            def _(n, s=s):
+            low, high = halves[h]
+            part = pl.ds(low * tile, (high - low) * tile)
+
+            @pl.loop(0, mg * rows // block)
+            def _(g, s=s, part=part):
+                chunk = pl.ds(pl.multiple_of(g * block, block), block)
+                raised[chunk, pl.ds(0, part.size)] = jnp.dot(
+                    xs[chunk, :], wm[s, :, part], preferred_element_type=F32
+                ).astype(BF16)
+
+            @pl.loop(low, high)
+            def _(n, s=s, low=low):
                 here = pl.ds(pl.multiple_of(n * tile, tile), tile)
                 whole = pl.ds(pl.multiple_of(s * ts + n * tile, 128), tile)
-                coarse = jnp.dot(xs[...], wm[s, :, here], preferred_element_type=F32)
-                coarse = coarse.astype(BF16).astype(F32)
+                there = pl.ds(pl.multiple_of((n - low) * tile, tile), tile)
                 for t in range(tg):
                     re = im = None
                     for j in range(4):
@@ -337,8 +348,8 @@
                         turn = pl.ds(i, 1)
                         c = tcos[turn, whole]
                         d = tsin[turn, whole]
-                        u = coarse[i * rows : i * rows + rhs]
-                        v = coarse[i * rows + rhs : (i + 1) * rows]
+                        u = raised[pl.ds(i * rows, rhs), there].astype(F32)
+                        v = raised[pl.ds(i * rows + rhs, rhs), there].astype(F32)
                         a, b = c * u - d * v, d * u + c * v
                         re, im = (a, b) if re is None else (re + a, im + b)
                     gat[s, box, t, 0, :, here] = re.astype(BF16)
@@ -351,6 +362,7 @@
     order = visit_order(sectors)
     edge_copies = neighbour_copies(esl, esr, erl, err, ed_send, ed_recv)
     out_copies = []
+    depth = 384 if spanm % 384 == 0 else 128
     mfirst = rank.shape[0] - nb * mg + box * mg
     for step, s in enumerate(order):
         slot = step % 2
@@ -401,15 +413,20 @@
                         turned[i, 0] = (c * re + d * im).astype(BF16)
                         turned[i, 1] = (c * im - d * re).astype(BF16)
                 for m in range(mg):
-                    spread[pl.ds(m * rows, rows), :] = turned[
+                    spread[pl.ds(m * rows, rows), here] = turned[
                         rank[mfirst + m]
                     ].reshape(rows, tile)
-                acc[:, :, :, pl.ds(s * ms, spanm)] += lax.dot_general(
-                    spread[...],
-                    wm[s, :, here],
-                    (((1,), (1,)), ((), ())),
-                    preferred_element_type=F32,
-                ).reshape(mg, 2, rhs, spanm)
+
+        @pl.loop(0, spanm // depth)
+        def _(n, s=s):
+            back = pl.ds(pl.multiple_of(n * depth, depth), depth)
+            target = pl.ds(pl.multiple_of(s * ms + n * depth, 128), depth)
+            acc[:, :, :, target] += lax.dot_general(
+                spread[...],
+                wm[s, back, :],
+                (((1,), (1,)), ((), ())),
+                preferred_element_type=F32,
+            ).reshape(mg, 2, rhs, depth)
 
         out = pltpu.make_async_copy(
             stage.at[slot],
@@ -551,7 +568,8 @@
             pltpu.VMEM((2 * kinds, tblock), BF16),
             pltpu.VMEM((tg * nt * 2, tile), F32),
             pltpu.VMEM((mg, 2, rhs, tile), BF16),
-            pltpu.VMEM((mg * rows, tile), BF16),
+            pltpu.VMEM((mg * rows, (ts // tile + 1) // 2 * tile), BF16),
+            pltpu.VMEM((mg * rows, ts), BF16),
             pltpu.VMEM((mg, 2, rhs, mblock + 2 * EDGE), F32),
             pltpu.VMEM((2, tg, 2, rhs, ts), F32),
             pltpu.VMEM((mg, 2, rhs, EDGE), BF16),

time: 148 us -> 140 us (0.946)
  Pallas kernels: 134 us -> 126 us
    pallas_call x1, Pallas kernels: 134 us -> 126 us  [per_device(): pl.pallas_call(kernel, out_shape=(jax.ShapeDtypeStruct((tg, 2, rhs, tbloc...]
where the time goes in v2:
time: 140 us
  Pallas kernels  126 us (90%)
  local copies, waits for them, and re-layouts  7.39 us (5%)
  other arithmetic  4.15 us (3%)
  matrix products  1.45 us (1%)
    pallas_call x1, Pallas kernels, per_device(): pl.pallas_call(kernel, out_shape=(jax.ShapeDtypeStruct((tg, 2, rhs, tbloc...  126 us
    unnamed x4, local copies, waits for them, and re-layouts  5.95 us

profile of v2, /device:TPU:0, one launch (start us, length us, event | category | flops | bytes accessed | tf_op | source)
XLA Modules:
  0.0 140.1 jit_solution(16714129141198460163)
XLA Ops:
  0.7 0.7 and_select_fusion.2
  1.3 0.7 broadcast_add_fusion
  2.0 0.7 pad_add_fusion
  2.7 0.2 convert_reduce_fusion
  2.8 0.6 fusion.14.rank
  3.4 0.7 pad_add_fusion.1
  4.1 0.2 fusion.4
  4.3 0.5 fusion.16.child
  4.8 0.1 slice_bitcast_fusion
  4.9 0.7 copy.18.mpos
  5.6 1.4 %fusion.cnt = bf16[32,128]{1,0:T(8,128)(2,1)} fusion(s32[128]{0:T(128)S(1)} %get-tuple-element.4, s32[64]{0:T(128)} %param.25, s32[64]{0:T(128)S(1)} %and_select_fusion.2, s32[128]{0:T(128)S(1)} %get-tuple-element.5, s32[32]{0:T(128)S(1)} %get-tuple-element.6, s32[32]{0:T(128)S(1)} %get-tuple-element.7), kind=kOutput, calls=%fused_computation.1 | convolution fusion | flops 546816 | bytes 9984 | tf_op jit(solution)/shard_map/dot_general | solution.py:486
  7.0 0.7 copy.17.fpos
  7.7 126.5 %shard_map.140 = (f32[2,2,16,13312]{3,2,1,0:T(8,128)}, f32[8,2,16,3584]{3,2,1,0:T(8,128)}) custom-call(s32[40]{0:T(128)} %fusion.16.child, s32[160]{0:T(256)} %fusion.14.rank, bf16[4,2,16,8192]{3,2,1,0:T(8,128)(2,1)} %fine.1, bf16[4,384,896]{2,1,0:T(8,128)(2,1)} %fint.1, bf16[4,1024,3328]{2,1,0:T(8,128)(2,1)} %mint.1, bf16[64,2,13312]{2,1,0:T(2,128)(2,1)} %trans.1, ...), custom_call_target="tpu_custom_call" | custom-call | tf_op jit(solution)/shard_map/pallas_call | solution.py:544
  134.2 0.0 copy-start
  134.2 4.1 %copy.21 = f32[2,2,16,13312]{3,2,1,0:T(8,128)} copy(f32[2,2,16,13312]{3,2,1,0:T(8,128)} %get-tuple-element.10) | data formatting | bytes 6815744
  138.3 0.0 copy-done
  138.3 1.8 %copy.22 = f32[8,2,16,3584]{3,2,1,0:T(8,128)} copy(f32[8,2,16,3584]{3,2,1,0:T(8,128)S(1)} %copy-done) | data formatting | bytes 7340032
  (4 shorter events, 0.0 us)
Async XLA Ops:
  134.2 4.1 %copy-start = (f32[8,2,16,3584]{3,2,1,0:T(8,128)S(1)}, f32[8,2,16,3584]{3,2,1,0:T(8,128)}, u32[]{:S(2)}) copy-start(f32[8,2,16,3584]{3,2,1,0:T(8,128)} %get-tuple-element.11) | copy-start | bytes 11010052

commit v3 on v2

--- a/solution.py
+++ b/solution.py
@@ -382,25 +382,29 @@
                 whole = pl.ds(pl.multiple_of(s * ts + n * tile, 128), tile)
                 product = jnp.dot(cnt[...], tview[:, whole], preferred_element_type=F32)
                 cpl[...] = product.astype(BF16).astype(F32)
-                for t in range(tg):
-
-                    def add(u, total, t=t):
-                        re, im = total
-                        origin = u // tg
-                        q = u - origin * tg
+
+                def add(u, totals):
+                    origin = u // tg
+                    q = u - origin * tg
+                    a = gat[s, origin, q, 0, :, here].astype(F32)
+                    b = gat[s, origin, q, 1, :, here].astype(F32)
+                    sums = []
+                    for t in range(tg):
+                        re, im = totals[t]
                         c = cpl[pl.ds(2 * (t * nt + u), 1), :]
                         d = cpl[pl.ds(2 * (t * nt + u) + 1, 1), :]
-                        a = gat[s, origin, q, 0, :, here].astype(F32)
-                        b = gat[s, origin, q, 1, :, here].astype(F32)
-                        return re + (c * a - d * b), im + (c * b + d * a)
-
-                    total = (jnp.zeros((rhs, tile), F32), jnp.zeros((rhs, tile), F32))
-                    if nt <= 8:
-                        for u in range(nt):
-                            total = add(u, total)
-                    else:
-                        total = lax.fori_loop(0, nt, add, total)
-                    re, im = total
+                        sums.append((re + (c * a - d * b), im + (c * b + d * a)))
+                    return tuple(sums)
+
+                nothing = jnp.zeros((rhs, tile), F32)
+                totals = ((nothing, nothing),) * tg
+                if nt <= 8:
+                    for u in range(nt):
+                        totals = add(u, totals)
+                else:
+                    totals = lax.fori_loop(0, nt, add, totals)
+                for t in range(tg):
+                    re, im = totals[t]
                     stage[slot, t, 0, :, here] = re
                     stage[slot, t, 1, :, here] = im
                     re = re.astype(BF16).astype(F32)

time: 140 us -> 140 us (level)
  no operation moved by 1% of the time
where the time goes in v3:
time: 140 us
  Pallas kernels  126 us (90%)
  local copies, waits for them, and re-layouts  7.39 us (5%)
  other arithmetic  4.15 us (3%)
  matrix products  1.45 us (1%)
    pallas_call x1, Pallas kernels, per_device(): pl.pallas_call(kernel, out_shape=(jax.ShapeDtypeStruct((tg, 2, rhs, tbloc...  126 us
    unnamed x4, local copies, waits for them, and re-layouts  5.95 us

profile of v3, /device:TPU:0, one launch (start us, length us, event | category | flops | bytes accessed | tf_op | source)
XLA Modules:
  0.0 139.8 jit_solution(8573164984204328060)
XLA Ops:
  0.7 0.7 and_select_fusion.2
  1.3 0.7 broadcast_add_fusion
  2.0 0.7 pad_add_fusion
  2.7 0.2 convert_reduce_fusion
  2.8 0.6 fusion.14.rank
  3.4 0.7 pad_add_fusion.1
  4.1 0.2 fusion.4
  4.3 0.5 fusion.16.child
  4.8 0.1 slice_bitcast_fusion
  4.9 0.7 copy.18.mpos
  5.6 1.4 %fusion.cnt = bf16[32,128]{1,0:T(8,128)(2,1)} fusion(s32[128]{0:T(128)S(1)} %get-tuple-element.4, s32[64]{0:T(128)} %param.25, s32[64]{0:T(128)S(1)} %and_select_fusion.2, s32[128]{0:T(128)S(1)} %get-tuple-element.5, s32[32]{0:T(128)S(1)} %get-tuple-element.6, s32[32]{0:T(128)S(1)} %get-tuple-element.7), kind=kOutput, calls=%fused_computation.1 | convolution fusion | flops 546816 | bytes 9984 | tf_op jit(solution)/shard_map/dot_general | solution.py:490
  7.0 0.7 copy.17.fpos
  7.7 126.2 %shard_map.140 = (f32[2,2,16,13312]{3,2,1,0:T(8,128)}, f32[8,2,16,3584]{3,2,1,0:T(8,128)}) custom-call(s32[40]{0:T(128)} %fusion.16.child, s32[160]{0:T(256)} %fusion.14.rank, bf16[4,2,16,8192]{3,2,1,0:T(8,128)(2,1)} %fine.1, bf16[4,384,896]{2,1,0:T(8,128)(2,1)} %fint.1, bf16[4,1024,3328]{2,1,0:T(8,128)(2,1)} %mint.1, bf16[64,2,13312]{2,1,0:T(2,128)(2,1)} %trans.1, ...), custom_call_target="tpu_custom_call" | custom-call | tf_op jit(solution)/shard_map/pallas_call | solution.py:548
  133.9 0.0 copy-start
  133.9 4.1 %copy.21 = f32[2,2,16,13312]{3,2,1,0:T(8,128)} copy(f32[2,2,16,13312]{3,2,1,0:T(8,128)} %get-tuple-element.10) | data formatting | bytes 6815744
  138.0 0.0 copy-done
  138.0 1.8 %copy.22 = f32[8,2,16,3584]{3,2,1,0:T(8,128)} copy(f32[8,2,16,3584]{3,2,1,0:T(8,128)S(1)} %copy-done) | data formatting | bytes 7340032
  (4 shorter events, 0.0 us)
Async XLA Ops:
  133.9 4.1 %copy-start = (f32[8,2,16,3584]{3,2,1,0:T(8,128)S(1)}, f32[8,2,16,3584]{3,2,1,0:T(8,128)}, u32[]{:S(2)}) copy-start(f32[8,2,16,3584]{3,2,1,0:T(8,128)} %get-tuple-element.11) | copy-start | bytes 11010052
